TPU v7x, 512 devices: a whole 4x4x16 slice. The times are simulated.
512 devices in a mesh: seq: 128 (over z, y, core), grp: 4 (over x).
Axes of the slice: x: 4, y: 4, z: 16, core: 2. Of those that a mesh axis runs over, the one named last changes fastest.
Arguments:
- tokens: bfloat16 [131072, 512], P('seq'), may hold values from -12 to 12
- w_qkv: bfloat16 [3, 512, 512], P(None, None, 'grp'), may hold values from -0.25 to 0.25
- w_out: bfloat16 [512, 512], replicated, may hold values from -0.75 to 0.75
- w_up: bfloat16 [512, 2048], P(None, 'grp'), may hold values from -0.25 to 0.25
- w_down: bfloat16 [2048, 512], P('grp'), may hold values from -0.125 to 0.125
- score_scale: float32 [8], P('grp'), may hold values from 8 to 400
- patch_list: int32 [128, 3], P('seq'), may hold values from 0 to 127, as said below
- relay_dest: int32 [131072, 1], P('seq'), may hold values from 0 to 127; in each aligned block of 1024 rows (0 to 1023, 1024 to 2047, ...) at most 16 rows name the same one
Outputs:
- relayed: bfloat16 [262144, 512], P('seq', 'grp')
Inputs may be any that keep to these rules, and one draw needn't show every extreme that they name: `patch_list`: row p lists patch p first, then 3 - 1 other distinct patches, each at most 2 patches away from p. `relay_dest`: the rows of one block of 1024 tokens name any one block at most 16 times; in every draw some block names some block exactly 16 times.
All inputs are finite; a program needn't handle non-finite values.
Results may differ from a plain program's by a relative error of at most 0.017.
Values may be sent and summed in bfloat16 or wider, within the bound.
A program may use at most 64 MiB of HBM per device.

v0:
```python
import jax
import jax.numpy as jnp
from jax import lax
from jax.sharding import PartitionSpec as P

PATCH = 1024
REACH = 2
NB = 3


def shifted(block, axis, distance):
    devices = range(lax.axis_size(axis))
    route = [(i - distance, i) for i in devices if i - distance in devices]
    return lax.ppermute(block, axis, route)


def layer_norm(token_rows):
    row_mean = jnp.mean(token_rows, axis=-1, keepdims=True)
    spread = jnp.mean(token_rows * token_rows, axis=-1, keepdims=True) - row_mean * row_mean
    return (token_rows - row_mean) * lax.rsqrt(spread + 1e-05)


def unit_heads(values, head_dim):
    shaped = values.reshape(values.shape[0], -1, head_dim)
    scaled = shaped * lax.rsqrt(jnp.mean(shaped * shaped, axis=-1, keepdims=True) + 1e-06)
    return scaled.reshape(values.shape)


def project(token_rows, weights):
    normed = layer_norm(token_rows.astype(jnp.float32)).astype(jnp.bfloat16)
    return jnp.einsum("nd,cde->cne", normed, weights, preferred_element_type=jnp.float32)


def body(tokens, w_qkv, w_out, w_up, w_down, score_scale, patch_list, relay_dest):
    n_seq = lax.axis_size("seq")
    seq_index = lax.axis_index("seq")
    grp_index = lax.axis_index("grp")
    tok_dev, model_width = tokens.shape
    quarter = w_qkv.shape[2]
    heads_dev = score_scale.shape[0]
    head_dim = quarter // heads_dev
    patch_dev = tok_dev // PATCH
    hop_count = -(-REACH // patch_dev)
    offsets = [offset for offset in range(-hop_count, hop_count + 1) if offset != 0]
    own_products = project(tokens, w_qkv)
    queries = unit_heads(own_products[0], head_dim).astype(jnp.bfloat16)
    key_rows = unit_heads(own_products[1], head_dim).astype(jnp.bfloat16)
    value_rows = own_products[2].astype(jnp.bfloat16)
    fetched_pairs = [shifted((key_rows, value_rows), "seq", -offset) for offset in offsets]
    near_keys = [fetched_pair[0] for fetched_pair in fetched_pairs]
    near_values = [fetched_pair[1] for fetched_pair in fetched_pairs]
    window_keys = jnp.concatenate(near_keys[:hop_count] + [key_rows] + near_keys[hop_count:], 0)
    window_values = jnp.concatenate(
        near_values[:hop_count] + [value_rows] + near_values[hop_count:], 0
    )
    window_count = 2 * hop_count + 1
    key_patches = window_keys.reshape(window_count * patch_dev, PATCH, quarter)
    value_patches = window_values.reshape(window_count * patch_dev, PATCH, quarter)
    first_patch = (seq_index - hop_count) * patch_dev
    relative = patch_list - first_patch
    listed_keys = key_patches[relative].reshape(patch_dev, NB * PATCH, quarter)
    listed_values = value_patches[relative].reshape(patch_dev, NB * PATCH, quarter)
    block_rows = min(512, PATCH)
    block_count = PATCH // block_rows
    query_blocks = queries.reshape(patch_dev, block_count, block_rows, quarter)
    factors = score_scale / head_dim

    def attend(item_index):
        patch_index = item_index // (heads_dev * block_count)
        head_index = item_index // block_count % heads_dev
        block_index = item_index % block_count
        query_block = lax.dynamic_slice_in_dim(
            query_blocks[patch_index, block_index], head_index * head_dim, head_dim, 1
        )
        key_block = lax.dynamic_slice_in_dim(
            listed_keys[patch_index], head_index * head_dim, head_dim, 1
        )
        value_block = lax.dynamic_slice_in_dim(
            listed_values[patch_index], head_index * head_dim, head_dim, 1
        )
        scores = lax.dot_general(
            query_block, key_block, (((1,), (1,)), ((), ())), preferred_element_type=jnp.float32
        )
        scores = scores * factors[head_index]
        row_top = jnp.max(scores, axis=1, keepdims=True)
        exponent = jnp.exp(scores - row_top)
        row_total = jnp.sum(exponent, axis=1, keepdims=True)
        weighted = jnp.dot(
            exponent.astype(jnp.bfloat16), value_block, preferred_element_type=jnp.float32
        )
        return (weighted / row_total).astype(jnp.bfloat16)

    attended = lax.map(attend, jnp.arange(patch_dev * heads_dev * block_count, dtype=jnp.int32))
    attended = attended.reshape(patch_dev, heads_dev, block_count, block_rows, head_dim)
    attended = attended.transpose(0, 2, 3, 1, 4).reshape(tok_dev, quarter)
    head_weights = lax.dynamic_slice_in_dim(w_out, grp_index * quarter, quarter, 0)
    partial_proj = jnp.dot(attended, head_weights, preferred_element_type=jnp.float32)
    proj_share = lax.psum_scatter(
        partial_proj.astype(jnp.bfloat16), "grp", scatter_dimension=1, tiled=True
    ).astype(jnp.float32)
    token_share = lax.dynamic_slice_in_dim(tokens, grp_index * quarter, quarter, 1).astype(
        jnp.float32
    )
    resid = (token_share + proj_share).astype(jnp.bfloat16)
    resid_wide = resid.astype(jnp.float32)
    row_sums = lax.psum(
        (jnp.sum(resid_wide, axis=1), jnp.sum(resid_wide * resid_wide, axis=1)), "grp"
    )
    row_mean = row_sums[0] / model_width
    spread = row_sums[1] / model_width - row_mean * row_mean
    normed_share = ((resid_wide - row_mean[:, None]) * lax.rsqrt(spread + 1e-05)[:, None]).astype(
        jnp.bfloat16
    )
    hidden_pre = jnp.dot(
        lax.all_gather(normed_share, "grp", axis=1, tiled=True),
        w_up,
        preferred_element_type=jnp.float32,
    )
    hidden = jax.nn.gelu(hidden_pre).astype(jnp.bfloat16)
    partial_down = jnp.dot(hidden, w_down, preferred_element_type=jnp.float32)
    down_share = lax.psum_scatter(
        partial_down.astype(jnp.bfloat16), "grp", scatter_dimension=1, tiled=True
    ).astype(jnp.float32)
    out_rows = (resid.astype(jnp.float32) + down_share).astype(jnp.bfloat16)
    capacity = 2 * tok_dev // n_seq
    destination = relay_dest[:, 0]
    onehot = (destination[:, None] == jnp.arange(n_seq, dtype=jnp.int32)[None, :]).astype(jnp.int32)
    before = jnp.cumsum(onehot, axis=0) - onehot
    rank_rows = jnp.sum(before * onehot, axis=1)
    slot_index = destination * capacity + rank_rows
    send_buffer = jnp.zeros((n_seq * capacity, quarter), jnp.bfloat16).at[slot_index].set(out_rows)
    received = lax.all_to_all(
        send_buffer.reshape(n_seq, capacity, quarter),
        "seq",
        split_axis=0,
        concat_axis=0,
        tiled=True,
    )
    return received.reshape(n_seq * capacity, quarter)


def solution(mesh):
    return jax.shard_map(
        body,
        mesh=mesh,
        in_specs=(
            P("seq", None),
            P(None, None, "grp"),
            P(),
            P(None, "grp"),
            P("grp", None),
            P("grp"),
            P("seq", None),
            P("seq", None),
        ),
        out_specs=P("seq", "grp"),
        check_vma=False,
    )
```

profile of v0, /device:TPU:33, one launch (start us, length us, event | category | flops | bytes accessed | tf_op | source)
XLA Modules:
  0.0 282.7 jit_solution(186942135605513350)
XLA Ops:
  6.5 1.6 convert_reduce_fusion
  8.2 1.2 copy.24
  9.4 2.0 fusion.36
  11.4 1.2 slice_multiply_fusion
  12.5 1.1 reduce_sum.83
  13.7 3.2 %collective-permute-start = (bf16[1024,128]{0,1:T(8,128)(2,1)S(1)}, bf16[1024,128]{0,1:T(8,128)(2,1)}, u32[]{:S(2)}, u32[]{:S(2)}) collective-permute-start(bf16[1024,128]{0,1:T(8,128)(2,1)S(1)} %fusion.50), channel_id=1, source_target_pairs={{0,8},{4,12},{8,16},{12,20},{16,24},{20,28},{24,32},{28,36},{32,40... | collective-permute-start | bytes 786440 | tf_op jit(solution)/shard_map/ppermute | solution.py:14
  16.9 4.0 %collective-permute-start.1 = (bf16[1024,128]{0,1:T(8,128)(2,1)S(1)}, bf16[1024,128]{0,1:T(8,128)(2,1)}, u32[]{:S(2)}, u32[]{:S(2)}) collective-permute-start(bf16[1024,128]{0,1:T(8,128)(2,1)S(1)} %fusion.50), channel_id=1, source_target_pairs={{0,4},{4,8},{8,12},{12,16},{16,20},{20,24},{24,28},{28,32},{32,36}... | collective-permute-start | bytes 786440 | tf_op jit(solution)/shard_map/ppermute | solution.py:14
  21.0 1.9 collective-permute-start.2
  22.9 4.2 %collective-permute-start.3 = (bf16[1024,128]{0,1:T(8,128)(2,1)S(1)}, bf16[1024,128]{0,1:T(8,128)(2,1)}, u32[]{:S(2)}, u32[]{:S(2)}) collective-permute-start(bf16[1024,128]{0,1:T(8,128)(2,1)S(1)} %fusion.50), channel_id=1, source_target_pairs={{8,0},{12,4},{16,8},{20,12},{24,16},{28,20},{32,24},{36,28},{40,32... | collective-permute-start | bytes 786440 | tf_op jit(solution)/shard_map/ppermute | solution.py:14
  27.9 1.9 collective-permute-start.4
  31.2 3.9 %collective-permute-start.5 = (bf16[1024,128]{0,1:T(8,128)(2,1)}, bf16[1024,128]{0,1:T(8,128)(2,1)S(1)}, u32[]{:S(2)}, u32[]{:S(2)}) collective-permute-start(bf16[1024,128]{0,1:T(8,128)(2,1)} %fusion.53), channel_id=1, source_target_pairs={{0,4},{4,8},{8,12},{12,16},{16,20},{20,24},{24,28},{28,32},{32,36}... | collective-permute-start | bytes 786440 | tf_op jit(solution)/shard_map/ppermute | solution.py:14
  35.1 1.0 constant_dynamic-update-slice_fusion.4
  36.1 2.3 collective-permute-start.6
  38.4 1.0 constant_dynamic-update-slice_fusion.3
  39.4 5.4 %collective-permute-start.7 = (bf16[1024,128]{0,1:T(8,128)(2,1)}, bf16[1024,128]{0,1:T(8,128)(2,1)S(1)}, u32[]{:S(2)}, u32[]{:S(2)}) collective-permute-start(bf16[1024,128]{0,1:T(8,128)(2,1)} %fusion.53), channel_id=1, source_target_pairs={{8,0},{12,4},{16,8},{20,12},{24,16},{28,20},{32,24},{36,28},{40,32... | collective-permute-start | bytes 786440 | tf_op jit(solution)/shard_map/ppermute | solution.py:14
  44.8 1.7 constant_dynamic-update-slice_fusion.9
  47.4 1.0 constant_dynamic-update-slice_fusion
  48.4 1.0 copy-done.2
  50.2 1.8 copy.25
  52.0 1.8 constant_dynamic-update-slice_fusion.7
  55.4 2.4 copy.26
  58.5 2.0 gather_fusion.1
  60.5 39.8 %while.13 = (s32[]{:T(128)}, bf16[4,512,64]{1,2,0:T(8,128)(2,1)S(1)}, s32[4]{0:T(128)S(1)}, bf16[1,2,512,128]{2,1,3,0:T(2,128)(2,1)S(1)}, bf16[1,3072,128]{2,1,0...) while((s32[]{:T(128)}, ...), condition=%wide.region_10.11_spmd, body=%wide.region_7.10_spmd.sunk | while | flops 415300672 | bytes 20851312 | solution.py:93
  64.7 1.8 multiply_reduce_fusion.2
  66.5 1.8 fusion.78
  68.3 2.2 fusion.79
  74.6 1.8 multiply_reduce_fusion.2
  76.4 1.8 fusion.78
  78.2 2.2 fusion.79
  84.6 1.8 multiply_reduce_fusion.2
  86.4 1.8 fusion.78
  88.2 2.2 fusion.79
  94.6 1.8 multiply_reduce_fusion.2
  96.4 1.8 fusion.78
  98.2 2.2 fusion.79
  101.2 1.3 copy.29
  102.6 34.9 %reduce-scatter.7.cloned.1.call-done = bf16[128,1024]{1,0:T(8,128)(2,1)} async-done(((bf16[512,1024]{1,0:T(8,128)(2,1)}), bf16[128,1024]{1,0:T(8,128)(2,1)}) %reduce-scatter.7.cloned.1.call-update) | async-done | bytes 262160
  137.5 1.1 copy.30
  138.7 1.3 convert_reduce_fusion.1
  140.0 6.6 %all-reduce = (f32[1024]{0:T(1024)S(1)}, f32[1024]{0:T(1024)S(1)}) all-reduce(f32[1024]{0:T(1024)S(1)} %get-tuple-element.144, f32[1024]{0:T(1024)S(1)} %get-tuple-element.143), channel_id=1, replica_groups=mesh['seq'=128,'grp'=4] {'grp'}, use_global_device_ids=true, to_apply=%region_15.16 | all-reduce | flops 2048 | bytes 16384 | tf_op jit(solution)/shard_map/psum | solution.py:106
  146.6 1.0 fusion.45
  147.9 35.5 %all-gather.2.cloned.1.call-done = bf16[1024,512]{1,0:T(8,128)(2,1)} async-done(((bf16[1024,128]{1,0:T(8,128)(2,1)}), bf16[1024,512]{1,0:T(8,128)(2,1)}) %all-gather.2.cloned.1.call-update) | async-done | bytes 1048592 | tf_op jit(solution)/shard_map/all_gather | solution.py:115
  183.4 2.7 convolution_convert_fusion.1
  186.1 1.3 copy.31
  188.4 31.1 %reduce-scatter.9.cloned.1.call-done = bf16[128,1024]{1,0:T(8,128)(2,1)} async-done(((bf16[512,1024]{1,0:T(8,128)(2,1)}), bf16[128,1024]{1,0:T(8,128)(2,1)}) %reduce-scatter.9.cloned.1.call-update) | async-done | bytes 262160
  219.5 1.1 copy.32
  220.6 3.4 %scatter_custom_fusion = bf16[2048,128]{1,0:T(8,128)(2,1)S(1)} fusion(s32[1024]{0:T(1024)S(1)} %bitcast.114, bf16[1024,128]{1,0:T(8,128)(2,1)S(1)} %get-tuple-element.161, bf16[1024,128]{1,0:T(8,128)(2,1)S(1)} %copy.32, bf16[]{:T(256)} %constant.173.clone.1), kind=kCustom, calls=%fused_computation.67 | custom fusion | flops 524288 | bytes 1048578 | tf_op jit(solution)/shard_map/scatter | solution.py:131
  224.0 51.4 %all_to_all.5 = bf16[128,16,128]{2,1,0:T(8,128)(2,1)S(1)} all-to-all(bf16[128,16,128]{2,1,0:T(8,128)(2,1)S(1)} %bitcast.103), channel_id=1, replica_groups=mesh['seq'=128,'grp'=4] {'seq'}, dimensions={0} | all-to-all | bytes 1048576 | tf_op jit(solution)/shard_map/all_to_all | solution.py:132
  (80 shorter events, 14.7 us)
Async XLA Ops:
  6.5 94.2 %copy-start = (bf16[512,512]{1,0:T(8,128)(2,1)S(1)}, bf16[512,512]{1,0:T(8,128)(2,1)}, u32[]{:S(2)}) copy-start(bf16[512,512]{1,0:T(8,128)(2,1)} %param.12) | copy-start | bytes 1572868
  6.5 131.0 %reduce-scatter.7.cloned.1.call-start = ((), (), s32[]{:S(2)}) async-start(), calls=%async_computation.4 | async-start | bytes 1310720
  11.4 16.5 %copy-start.1 = (f32[1024,384]{0,1}, f32[1024,384]{0,1:S(1)}, u32[]{:S(2)}) copy-start(f32[1024,384]{0,1:S(1)} %fusion.36) | copy-start | bytes 4718596
  13.7 17.2 %copy-start.6 = (f32[2]{0:T(128)S(1)}, f32[2]{0:T(128)}, u32[]{:S(2)}) copy-start(f32[2]{0:T(128)} %param.15) | copy-start | bytes 28
  13.7 17.5 %collective-permute-start = (bf16[1024,128]{0,1:T(8,128)(2,1)S(1)}, bf16[1024,128]{0,1:T(8,128)(2,1)}, u32[]{:S(2)}, u32[]{:S(2)}) collective-permute-start(bf16[1024,128]{0,1:T(8,128)(2,1)S(1)} %fusion.50), channel_id=1, source_target_pairs={{0,8},{4,12},{8,16},{12,20},{16,24},{20,28},{24,32},{28,36},{32,40... | collective-permute-start | bytes 786440 | tf_op jit(solution)/shard_map/ppermute | solution.py:14
  16.9 19.2 %collective-permute-start.1 = (bf16[1024,128]{0,1:T(8,128)(2,1)S(1)}, bf16[1024,128]{0,1:T(8,128)(2,1)}, u32[]{:S(2)}, u32[]{:S(2)}) collective-permute-start(bf16[1024,128]{0,1:T(8,128)(2,1)S(1)} %fusion.50), channel_id=1, source_target_pairs={{0,4},{4,8},{8,12},{12,16},{16,20},{20,24},{24,28},{28,32},{32,36}... | collective-permute-start | bytes 786440 | tf_op jit(solution)/shard_map/ppermute | solution.py:14
  21.0 25.5 %collective-permute-start.2 = (bf16[1024,128]{0,1:T(8,128)(2,1)S(1)}, bf16[1024,128]{0,1:T(8,128)(2,1)}, u32[]{:S(2)}, u32[]{:S(2)}) collective-permute-start(bf16[1024,128]{0,1:T(8,128)(2,1)S(1)} %fusion.50), channel_id=1, source_target_pairs={{4,0},{8,4},{12,8},{16,12},{20,16},{24,20},{28,24},{32,28},{36,32}... | collective-permute-start | bytes 786440 | tf_op jit(solution)/shard_map/ppermute | solution.py:14
  22.9 24.5 %collective-permute-start.3 = (bf16[1024,128]{0,1:T(8,128)(2,1)S(1)}, bf16[1024,128]{0,1:T(8,128)(2,1)}, u32[]{:S(2)}, u32[]{:S(2)}) collective-permute-start(bf16[1024,128]{0,1:T(8,128)(2,1)S(1)} %fusion.50), channel_id=1, source_target_pairs={{8,0},{12,4},{16,8},{20,12},{24,16},{28,20},{32,24},{36,28},{40,32... | collective-permute-start | bytes 786440 | tf_op jit(solution)/shard_map/ppermute | solution.py:14
  27.9 11.5 %collective-permute-start.4 = (bf16[1024,128]{0,1:T(8,128)(2,1)}, bf16[1024,128]{0,1:T(8,128)(2,1)}, u32[]{:S(2)}, u32[]{:S(2)}) collective-permute-start(bf16[1024,128]{0,1:T(8,128)(2,1)} %fusion.53), channel_id=1, source_target_pairs={{0,8},{4,12},{8,16},{12,20},{16,24},{20,28},{24,32},{28,36},{32,40... | collective-permute-start | bytes 786440 | tf_op jit(solution)/shard_map/ppermute | solution.py:14
  29.8 1.3 copy-start.7
  31.2 17.3 %collective-permute-start.5 = (bf16[1024,128]{0,1:T(8,128)(2,1)}, bf16[1024,128]{0,1:T(8,128)(2,1)S(1)}, u32[]{:S(2)}, u32[]{:S(2)}) collective-permute-start(bf16[1024,128]{0,1:T(8,128)(2,1)} %fusion.53), channel_id=1, source_target_pairs={{0,4},{4,8},{8,12},{12,16},{16,20},{20,24},{24,28},{28,32},{32,36}... | collective-permute-start | bytes 786440 | tf_op jit(solution)/shard_map/ppermute | solution.py:14
  36.1 17.7 %collective-permute-start.6 = (bf16[1024,128]{0,1:T(8,128)(2,1)}, bf16[1024,128]{0,1:T(8,128)(2,1)S(1)}, u32[]{:S(2)}, u32[]{:S(2)}) collective-permute-start(bf16[1024,128]{0,1:T(8,128)(2,1)} %fusion.53), channel_id=1, source_target_pairs={{4,0},{8,4},{12,8},{16,12},{20,16},{24,20},{28,24},{32,28},{36,32}... | collective-permute-start | bytes 786440 | tf_op jit(solution)/shard_map/ppermute | solution.py:14
  39.4 15.2 %collective-permute-start.7 = (bf16[1024,128]{0,1:T(8,128)(2,1)}, bf16[1024,128]{0,1:T(8,128)(2,1)S(1)}, u32[]{:S(2)}, u32[]{:S(2)}) collective-permute-start(bf16[1024,128]{0,1:T(8,128)(2,1)} %fusion.53), channel_id=1, source_target_pairs={{8,0},{12,4},{16,8},{20,12},{24,16},{28,20},{32,24},{36,28},{40,32... | collective-permute-start | bytes 786440 | tf_op jit(solution)/shard_map/ppermute | solution.py:14
  48.4 1.1 copy-start.2
  102.5 80.9 %copy-start.4 = (bf16[512,512]{1,0:T(8,128)(2,1)S(1)}, bf16[512,512]{1,0:T(8,128)(2,1)}, u32[]{:S(2)}) copy-start(bf16[512,512]{1,0:T(8,128)(2,1)} %param.14) | copy-start | bytes 1572868
  102.5 80.9 %copy-start.5 = (bf16[512,512]{1,0:T(8,128)(2,1)S(1)}, bf16[512,512]{1,0:T(8,128)(2,1)}, u32[]{:S(2)}) copy-start(bf16[512,512]{1,0:T(8,128)(2,1)} %param.13) | copy-start | bytes 1572868
  102.5 80.9 %all-gather.2.cloned.1.call-start = ((), (), s32[]{:S(2)}) async-start(), calls=%async_computation.3 | async-start | bytes 1310720 | tf_op jit(solution)/shard_map/all_gather | solution.py:115
  147.7 71.8 %reduce-scatter.9.cloned.1.call-start = ((), (), s32[]{:S(2)}) async-start(), calls=%async_computation.5 | async-start | bytes 1310720
  186.1 1.4 copy-start.3
Sparse Core Ops, SparseCore 0:
  102.7 34.8 reduce-scatter.6
  147.8 35.6 all-gather.1
  187.6 31.8 reduce-scatter.8
where the time goes:
time: 284 us; the launch traced here: 283 us
  waiting for transfers between devices  102 us (36%)
  blocking collectives  58 us (20%)
  local copies, waits for them, and re-layouts  32.6 us (11%)
  starting transfers between devices  27.1 us (10%)
  matrix products  21.2 us (7%)
  other arithmetic  17.8 us (6%)
  between operations  13.6 us (5%)
  loops' own time  10.7 us (4%)
    unnamed x5, waiting for transfers between devices  66.1 us
    all_to_all x1, blocking collectives, body(): lax.all_to_all(send_buffer.reshape(n_seq, capacity, quarter), 'seq', spli...  51.4 us
    all_gather x1, waiting for transfers between devices, body(): lax.all_gather(normed_share, 'grp', axis=1, tiled=True)  35.5 us
    ppermute x8, starting transfers between devices, shifted(): return lax.ppermute(block, axis, route)  26.9 us
    unnamed x31, local copies, waits for them, and re-layouts  15.9 us
    another operation x1, loops' own time, body(): lax.map(attend, jnp.arange(patch_dev * heads_dev * block_count, dtype=jnp...  10.7 us
    dot_general x4, matrix products, attend(): jnp.dot(exponent.astype(jnp.bfloat16), value_block, preferred_element_typ...  8.91 us
    dot_general x4, matrix products, attend(): lax.dot_general(query_block, key_block, (((1,), (1,)), ((), ())), preferr...  7.2 us
  transfers between devices with their start and end apart: 11, of which 3 were waited for; matrix products, arithmetic and copies ran while one was open for 5% of the time, Pallas kernels for 0%

commit v1 on v0

--- a/solution.py
+++ b/solution.py
@@ -6,6 +6,28 @@
 PATCH = 1024
 REACH = 2
 NB = 3
+
+
+def joined_along(blocks, dim):
+    blocks = jnp.moveaxis(blocks, 0, dim)
+    dims = blocks.shape
+    return blocks.reshape(*dims[:dim], dims[dim] * dims[dim + 1], *dims[dim + 2 :])
+
+
+def gather_around(x, axis, dim):
+    peers = lax.axis_size(axis)
+    pairs = [(i, (i + 1) % peers) for i in range(peers)]
+    back = [(b, a) for a, b in pairs]
+    lower, upper = ([], [])
+    for step in range(peers - 1):
+        if step % 2 == 0:
+            lower.append(lax.ppermute(lower[-1] if lower else x, axis, pairs))
+        else:
+            upper.append(lax.ppermute(upper[-1] if upper else x, axis, back))
+    blocks = jnp.stack([*lower[::-1], x, *upper])
+    shift = lax.axis_index(axis) - len(lower)
+    blocks = blocks[(jnp.arange(peers) - shift) % peers]
+    return joined_along(blocks, dim)
 
 
 def shifted(block, axis, distance):
@@ -112,9 +134,7 @@
         jnp.bfloat16
     )
     hidden_pre = jnp.dot(
-        lax.all_gather(normed_share, "grp", axis=1, tiled=True),
-        w_up,
-        preferred_element_type=jnp.float32,
+        gather_around(normed_share, "grp", 1), w_up, preferred_element_type=jnp.float32
     )
     hidden = jax.nn.gelu(hidden_pre).astype(jnp.bfloat16)
     partial_down = jnp.dot(hidden, w_down, preferred_element_type=jnp.float32)

time: 284 us -> 268 us (0.944)
  waiting for transfers between devices: 102 us -> 76.4 us
  starting transfers between devices: 27.1 us -> 35.5 us
    all_gather x1 -> x0, waiting for transfers between devices: 35.5 us -> none  [body(): lax.all_gather(normed_share, 'grp', axis=1, tiled=True)]
    ppermute x0 -> x3, starting transfers between devices: none -> 8.58 us  [the longest x2 4.94 us: gather_around(): lower.append(lax.ppermute(lower[-1] if lower else x, axis, pairs))]
    ppermute x0 -> x3, waiting for transfers between devices: none -> 7.65 us  [the longest x2 7.65 us: gather_around(): lower.append(lax.ppermute(lower[-1] if lower else x, axis, pairs))]
    unnamed x5 -> x4, waiting for transfers between devices: 66.1 us -> 68.7 us
    unnamed x31 -> x29, local copies, waits for them, and re-layouts: 15.9 us -> 15.9 us
  transfers between devices with their start and end apart: 11 -> 13, of which waited for: 3 -> 4; matrix products, arithmetic and copies ran while one was open for 5% -> 5% of each run, Pallas kernels for 0% -> 0%
where the time goes in v1:
time: 268 us; the launch traced here: 267 us
  waiting for transfers between devices  76.4 us (29%)
  blocking collectives  58.1 us (22%)
  starting transfers between devices  35.5 us (13%)
  local copies, waits for them, and re-layouts  33.9 us (13%)
  matrix products  21.1 us (8%)
  other arithmetic  17.6 us (7%)
  between operations  14 us (5%)
  loops' own time  10.7 us (4%)
    unnamed x4, waiting for transfers between devices  68.7 us
    all_to_all x1, blocking collectives, body(): lax.all_to_all(send_buffer.reshape(n_seq, capacity, quarter), 'seq', spli...  51.4 us
    ppermute x8, starting transfers between devices, shifted(): return lax.ppermute(block, axis, route)  26.9 us
    unnamed x29, local copies, waits for them, and re-layouts  15.9 us
    another operation x1, loops' own time, body(): lax.map(attend, jnp.arange(patch_dev * heads_dev * block_count, dtype=jnp...  10.7 us
    dot_general x4, matrix products, attend(): jnp.dot(exponent.astype(jnp.bfloat16), value_block, preferred_element_typ...  8.91 us
    ppermute x2, waiting for transfers between devices, gather_around(): lower.append(lax.ppermute(lower[-1] if lower else x, axis, pairs))  7.65 us
    dot_general x4, matrix products, attend(): lax.dot_general(query_block, key_block, (((1,), (1,)), ((), ())), preferr...  7.2 us
  transfers between devices with their start and end apart: 13, of which 4 were waited for; matrix products, arithmetic and copies ran while one was open for 5% of the time, Pallas kernels for 0%

profile of v1, /device:TPU:33, one launch (start us, length us, event | category | flops | bytes accessed | tf_op | source)
XLA Modules:
  0.0 267.2 jit_solution(10453139159636129725)
XLA Ops:
  6.5 1.6 convert_reduce_fusion
  8.2 1.2 copy.32
  9.4 2.0 fusion.36
  11.4 1.2 slice_multiply_fusion
  12.5 1.1 reduce_sum.83
  13.7 3.2 %collective-permute-start = (bf16[1024,128]{0,1:T(8,128)(2,1)S(1)}, bf16[1024,128]{0,1:T(8,128)(2,1)}, u32[]{:S(2)}, u32[]{:S(2)}) collective-permute-start(bf16[1024,128]{0,1:T(8,128)(2,1)S(1)} %fusion.50), channel_id=1, source_target_pairs={{0,8},{4,12},{8,16},{12,20},{16,24},{20,28},{24,32},{28,36},{32,40... | collective-permute-start | bytes 786440 | tf_op jit(solution)/shard_map/ppermute | solution.py:36
  16.9 4.0 %collective-permute-start.1 = (bf16[1024,128]{0,1:T(8,128)(2,1)S(1)}, bf16[1024,128]{0,1:T(8,128)(2,1)}, u32[]{:S(2)}, u32[]{:S(2)}) collective-permute-start(bf16[1024,128]{0,1:T(8,128)(2,1)S(1)} %fusion.50), channel_id=1, source_target_pairs={{0,4},{4,8},{8,12},{12,16},{16,20},{20,24},{24,28},{28,32},{32,36}... | collective-permute-start | bytes 786440 | tf_op jit(solution)/shard_map/ppermute | solution.py:36
  21.0 1.9 collective-permute-start.2
  22.9 4.2 %collective-permute-start.3 = (bf16[1024,128]{0,1:T(8,128)(2,1)S(1)}, bf16[1024,128]{0,1:T(8,128)(2,1)}, u32[]{:S(2)}, u32[]{:S(2)}) collective-permute-start(bf16[1024,128]{0,1:T(8,128)(2,1)S(1)} %fusion.50), channel_id=1, source_target_pairs={{8,0},{12,4},{16,8},{20,12},{24,16},{28,20},{32,24},{36,28},{40,32... | collective-permute-start | bytes 786440 | tf_op jit(solution)/shard_map/ppermute | solution.py:36
  27.9 1.9 collective-permute-start.4
  31.2 3.9 %collective-permute-start.5 = (bf16[1024,128]{0,1:T(8,128)(2,1)}, bf16[1024,128]{0,1:T(8,128)(2,1)S(1)}, u32[]{:S(2)}, u32[]{:S(2)}) collective-permute-start(bf16[1024,128]{0,1:T(8,128)(2,1)} %fusion.53), channel_id=1, source_target_pairs={{0,4},{4,8},{8,12},{12,16},{16,20},{20,24},{24,28},{28,32},{32,36}... | collective-permute-start | bytes 786440 | tf_op jit(solution)/shard_map/ppermute | solution.py:36
  36.1 2.3 collective-permute-start.6
  39.4 5.4 %collective-permute-start.7 = (bf16[1024,128]{0,1:T(8,128)(2,1)}, bf16[1024,128]{0,1:T(8,128)(2,1)S(1)}, u32[]{:S(2)}, u32[]{:S(2)}) collective-permute-start(bf16[1024,128]{0,1:T(8,128)(2,1)} %fusion.53), channel_id=1, source_target_pairs={{8,0},{12,4},{16,8},{20,12},{24,16},{28,20},{32,24},{36,28},{40,32... | collective-permute-start | bytes 786440 | tf_op jit(solution)/shard_map/ppermute | solution.py:36
  44.8 1.7 constant_dynamic-update-slice_fusion.9
  48.4 1.0 copy-done.2
  50.2 1.8 copy.33
  52.0 1.8 constant_dynamic-update-slice_fusion.7
  55.4 2.4 copy.34
  58.5 2.0 gather_fusion.1
  60.5 39.8 %while.13 = (s32[]{:T(128)}, bf16[4,512,64]{1,2,0:T(8,128)(2,1)S(1)}, s32[4]{0:T(128)S(1)}, bf16[1,2,512,128]{2,1,3,0:T(2,128)(2,1)S(1)}, bf16[1,3072,128]{2,1,0...) while((s32[]{:T(128)}, ...), condition=%wide.region_10.11_spmd, body=%wide.region_7.10_spmd.sunk | while | flops 415300672 | bytes 20851312 | solution.py:115
  64.7 1.8 multiply_reduce_fusion.2
  66.5 1.8 fusion.81
  68.3 2.2 fusion.82
  74.6 1.8 multiply_reduce_fusion.2
  76.4 1.8 fusion.81
  78.2 2.2 fusion.82
  84.6 1.8 multiply_reduce_fusion.2
  86.4 1.8 fusion.81
  88.2 2.2 fusion.82
  94.6 1.8 multiply_reduce_fusion.2
  96.4 1.8 fusion.81
  98.2 2.2 fusion.82
  101.2 1.3 copy.38
  102.6 34.9 %reduce-scatter.7.cloned.1.call-done = bf16[128,1024]{1,0:T(8,128)(2,1)} async-done(((bf16[512,1024]{1,0:T(8,128)(2,1)}), bf16[128,1024]{1,0:T(8,128)(2,1)}) %reduce-scatter.7.cloned.1.call-update) | async-done | bytes 262160
  137.5 1.1 copy.39
  138.7 1.3 convert_reduce_fusion.1
  140.0 6.6 %all-reduce = (f32[1024]{0:T(1024)S(1)}, f32[1024]{0:T(1024)S(1)}) all-reduce(f32[1024]{0:T(1024)S(1)} %get-tuple-element.151, f32[1024]{0:T(1024)S(1)} %get-tuple-element.150), channel_id=1, replica_groups=mesh['seq'=128,'grp'=4] {'grp'}, use_global_device_ids=true, to_apply=%region_15.16 | all-reduce | flops 2048 | bytes 16384 | tf_op jit(solution)/shard_map/psum | solution.py:128
  146.9 2.8 %collective-permute-start.8 = (bf16[1024,128]{1,0:T(8,128)(2,1)S(1)}, bf16[1024,128]{1,0:T(8,128)(2,1)S(1)}, u32[]{:S(2)}, u32[]{:S(2)}) collective-permute-start(bf16[1024,128]{1,0:T(8,128)(2,1)S(1)} %fusion.45), channel_id=1, source_target_pairs={{0,1},{1,2},{2,3},{3,0},{4,5},{5,6},{6,7},{7,4},{8,9},{9,10},{10,1... | collective-permute-start | bytes 786440 | tf_op jit(solution)/shard_map/ppermute | solution.py:24
  149.8 3.6 %collective-permute-start.10 = (bf16[1024,128]{1,0:T(8,128)(2,1)S(1)}, bf16[1024,128]{1,0:T(8,128)(2,1)S(1)}, u32[]{:S(2)}, u32[]{:S(2)}) collective-permute-start(bf16[1024,128]{1,0:T(8,128)(2,1)S(1)} %fusion.45), channel_id=1, source_target_pairs={{1,0},{2,1},{3,2},{0,3},{5,4},{6,5},{7,6},{4,7},{9,8},{10,9},{11,1... | collective-permute-start | bytes 786440 | tf_op jit(solution)/shard_map/ppermute | solution.py:26
  153.5 1.8 collective-permute-done.8
  155.3 2.1 collective-permute-start.9
  157.7 5.9 %collective-permute-done.9 = bf16[1024,128]{1,0:T(8,128)(2,1)S(1)} collective-permute-done((bf16[1024,128]{1,0:T(8,128)(2,1)S(1)}, bf16[1024,128]{1,0:T(8,128)(2,1)S(1)}, u32[]{:S(2)}, u32[]{:S(2)}) %collective-permute-start.9) | collective-permute-done | bytes 262176 | tf_op jit(solution)/shard_map/ppermute | solution.py:24
  165.0 2.5 convolution_convert_fusion.1
  167.6 1.3 copy.40
  169.9 33.7 %reduce-scatter.9.cloned.1.call-done = bf16[128,1024]{1,0:T(8,128)(2,1)} async-done(((bf16[512,1024]{1,0:T(8,128)(2,1)}), bf16[128,1024]{1,0:T(8,128)(2,1)}) %reduce-scatter.9.cloned.1.call-update) | async-done | bytes 262160
  203.6 1.1 copy.41
  204.7 3.4 %scatter_custom_fusion = bf16[2048,128]{1,0:T(8,128)(2,1)S(1)} fusion(s32[1024]{0:T(1024)S(1)} %bitcast.128, bf16[1024,128]{1,0:T(8,128)(2,1)S(1)} %get-tuple-element.168, bf16[1024,128]{1,0:T(8,128)(2,1)S(1)} %copy.41, bf16[]{:T(256)} %constant.188.clone.1), kind=kCustom, calls=%fused_computation.69 | custom fusion | flops 524288 | bytes 1048578 | tf_op jit(solution)/shard_map/scatter | solution.py:151
  208.1 51.4 %all_to_all.5 = bf16[128,16,128]{2,1,0:T(8,128)(2,1)S(1)} all-to-all(bf16[128,16,128]{2,1,0:T(8,128)(2,1)S(1)} %bitcast.113), channel_id=1, replica_groups=mesh['seq'=128,'grp'=4] {'seq'}, dimensions={0} | all-to-all | bytes 1048576 | tf_op jit(solution)/shard_map/all_to_all | solution.py:152
  (87 shorter events, 19.5 us)
Async XLA Ops:
  6.5 94.2 %copy-start = (bf16[512,512]{1,0:T(8,128)(2,1)S(1)}, bf16[512,512]{1,0:T(8,128)(2,1)}, u32[]{:S(2)}) copy-start(bf16[512,512]{1,0:T(8,128)(2,1)} %param.12) | copy-start | bytes 1572868
  6.5 131.0 %reduce-scatter.7.cloned.1.call-start = ((), (), s32[]{:S(2)}) async-start(), calls=%async_computation.3 | async-start | bytes 1310720
  11.4 16.5 %copy-start.1 = (f32[1024,384]{0,1}, f32[1024,384]{0,1:S(1)}, u32[]{:S(2)}) copy-start(f32[1024,384]{0,1:S(1)} %fusion.36) | copy-start | bytes 4718596
  13.7 17.2 %copy-start.5 = (f32[2]{0:T(128)S(1)}, f32[2]{0:T(128)}, u32[]{:S(2)}) copy-start(f32[2]{0:T(128)} %param.15) | copy-start | bytes 28
  13.7 17.5 %collective-permute-start = (bf16[1024,128]{0,1:T(8,128)(2,1)S(1)}, bf16[1024,128]{0,1:T(8,128)(2,1)}, u32[]{:S(2)}, u32[]{:S(2)}) collective-permute-start(bf16[1024,128]{0,1:T(8,128)(2,1)S(1)} %fusion.50), channel_id=1, source_target_pairs={{0,8},{4,12},{8,16},{12,20},{16,24},{20,28},{24,32},{28,36},{32,40... | collective-permute-start | bytes 786440 | tf_op jit(solution)/shard_map/ppermute | solution.py:36
  16.9 19.2 %collective-permute-start.1 = (bf16[1024,128]{0,1:T(8,128)(2,1)S(1)}, bf16[1024,128]{0,1:T(8,128)(2,1)}, u32[]{:S(2)}, u32[]{:S(2)}) collective-permute-start(bf16[1024,128]{0,1:T(8,128)(2,1)S(1)} %fusion.50), channel_id=1, source_target_pairs={{0,4},{4,8},{8,12},{12,16},{16,20},{20,24},{24,28},{28,32},{32,36}... | collective-permute-start | bytes 786440 | tf_op jit(solution)/shard_map/ppermute | solution.py:36
  21.0 25.5 %collective-permute-start.2 = (bf16[1024,128]{0,1:T(8,128)(2,1)S(1)}, bf16[1024,128]{0,1:T(8,128)(2,1)}, u32[]{:S(2)}, u32[]{:S(2)}) collective-permute-start(bf16[1024,128]{0,1:T(8,128)(2,1)S(1)} %fusion.50), channel_id=1, source_target_pairs={{4,0},{8,4},{12,8},{16,12},{20,16},{24,20},{28,24},{32,28},{36,32}... | collective-permute-start | bytes 786440 | tf_op jit(solution)/shard_map/ppermute | solution.py:36
  22.9 24.5 %collective-permute-start.3 = (bf16[1024,128]{0,1:T(8,128)(2,1)S(1)}, bf16[1024,128]{0,1:T(8,128)(2,1)}, u32[]{:S(2)}, u32[]{:S(2)}) collective-permute-start(bf16[1024,128]{0,1:T(8,128)(2,1)S(1)} %fusion.50), channel_id=1, source_target_pairs={{8,0},{12,4},{16,8},{20,12},{24,16},{28,20},{32,24},{36,28},{40,32... | collective-permute-start | bytes 786440 | tf_op jit(solution)/shard_map/ppermute | solution.py:36
  27.9 11.5 %collective-permute-start.4 = (bf16[1024,128]{0,1:T(8,128)(2,1)}, bf16[1024,128]{0,1:T(8,128)(2,1)}, u32[]{:S(2)}, u32[]{:S(2)}) collective-permute-start(bf16[1024,128]{0,1:T(8,128)(2,1)} %fusion.53), channel_id=1, source_target_pairs={{0,8},{4,12},{8,16},{12,20},{16,24},{20,28},{24,32},{28,36},{32,40... | collective-permute-start | bytes 786440 | tf_op jit(solution)/shard_map/ppermute | solution.py:36
  29.8 1.3 copy-start.6
  31.2 17.3 %collective-permute-start.5 = (bf16[1024,128]{0,1:T(8,128)(2,1)}, bf16[1024,128]{0,1:T(8,128)(2,1)S(1)}, u32[]{:S(2)}, u32[]{:S(2)}) collective-permute-start(bf16[1024,128]{0,1:T(8,128)(2,1)} %fusion.53), channel_id=1, source_target_pairs={{0,4},{4,8},{8,12},{12,16},{16,20},{20,24},{24,28},{28,32},{32,36}... | collective-permute-start | bytes 786440 | tf_op jit(solution)/shard_map/ppermute | solution.py:36
  36.1 17.7 %collective-permute-start.6 = (bf16[1024,128]{0,1:T(8,128)(2,1)}, bf16[1024,128]{0,1:T(8,128)(2,1)S(1)}, u32[]{:S(2)}, u32[]{:S(2)}) collective-permute-start(bf16[1024,128]{0,1:T(8,128)(2,1)} %fusion.53), channel_id=1, source_target_pairs={{4,0},{8,4},{12,8},{16,12},{20,16},{24,20},{28,24},{32,28},{36,32}... | collective-permute-start | bytes 786440 | tf_op jit(solution)/shard_map/ppermute | solution.py:36
  39.4 15.2 %collective-permute-start.7 = (bf16[1024,128]{0,1:T(8,128)(2,1)}, bf16[1024,128]{0,1:T(8,128)(2,1)S(1)}, u32[]{:S(2)}, u32[]{:S(2)}) collective-permute-start(bf16[1024,128]{0,1:T(8,128)(2,1)} %fusion.53), channel_id=1, source_target_pairs={{8,0},{12,4},{16,8},{20,12},{24,16},{28,20},{32,24},{36,28},{40,32... | collective-permute-start | bytes 786440 | tf_op jit(solution)/shard_map/ppermute | solution.py:36
  48.4 1.1 copy-start.2
  102.5 101.1 %reduce-scatter.9.cloned.1.call-start = ((), (), s32[]{:S(2)}) async-start(), calls=%async_computation.4 | async-start | bytes 1310720
  146.9 8.3 %collective-permute-start.8 = (bf16[1024,128]{1,0:T(8,128)(2,1)S(1)}, bf16[1024,128]{1,0:T(8,128)(2,1)S(1)}, u32[]{:S(2)}, u32[]{:S(2)}) collective-permute-start(bf16[1024,128]{1,0:T(8,128)(2,1)S(1)} %fusion.45), channel_id=1, source_target_pairs={{0,1},{1,2},{2,3},{3,0},{4,5},{5,6},{6,7},{7,4},{8,9},{9,10},{10,1... | collective-permute-start | bytes 786440 | tf_op jit(solution)/shard_map/ppermute | solution.py:24
  149.8 7.9 %collective-permute-start.10 = (bf16[1024,128]{1,0:T(8,128)(2,1)S(1)}, bf16[1024,128]{1,0:T(8,128)(2,1)S(1)}, u32[]{:S(2)}, u32[]{:S(2)}) collective-permute-start(bf16[1024,128]{1,0:T(8,128)(2,1)S(1)} %fusion.45), channel_id=1, source_target_pairs={{1,0},{2,1},{3,2},{0,3},{5,4},{6,5},{7,6},{4,7},{9,8},{10,9},{11,1... | collective-permute-start | bytes 786440 | tf_op jit(solution)/shard_map/ppermute | solution.py:26
  155.3 8.3 %collective-permute-start.9 = (bf16[1024,128]{1,0:T(8,128)(2,1)S(1)}, bf16[1024,128]{1,0:T(8,128)(2,1)S(1)}, u32[]{:S(2)}, u32[]{:S(2)}) collective-permute-start(bf16[1024,128]{1,0:T(8,128)(2,1)S(1)} %collective-permute-done.8), channel_id=1, source_target_pairs={{0,1},{1,2},{2,3},{3,0},{4,5},{5,6},{6,7},{7,4},{8,9},{9,10},{10,1... | collective-permute-start | bytes 786440 | tf_op jit(solution)/shard_map/ppermute | solution.py:24
  163.7 1.3 copy-start.4
  167.6 1.4 copy-start.3
Sparse Core Ops, SparseCore 0:
  102.7 34.8 reduce-scatter.6
  169.1 34.4 reduce-scatter.8
